TPU v7x, 512 devices: a whole 4x8x8 slice. The times are simulated.
512 devices in a mesh: pool: 4 (over x), ep: 128 (over y, z, core).
Axes of the slice: x: 4, y: 8, z: 8, core: 2. Of those that a mesh axis runs over, the one named last changes fastest.
Arguments:
- kv_pre: bfloat16 [262144, 576], P(('pool', 'ep')), may hold values from -6 to 6
- kv_gain: float32 [512], replicated, may hold values from 0.5 to 2
- send_list: int32 [512, 512, 1], P(('pool', 'ep')), may hold values from 0 to 511, as said below
- row_owner: int32 [262144], P(('pool', 'ep')), may hold values from 0 to 1
- queries: bfloat16 [1024, 128, 576], P(('pool', 'ep')), may hold values from -12 to 12
- cache: bfloat16 [1024, 1024, 576], P(('pool', 'ep')), may hold values from -4 to 4
- ctx_len: int32 [1024], P(('pool', 'ep')), may hold values from 2 to 1024, as said below
- value_up: bfloat16 [128, 512, 128], P('ep'), may hold values from -1.5 to 1.5
Outputs:
- head_values: bfloat16 [1024, 128, 128], P(('pool', 'ep'))
Inputs may be any that keep to these rules, and one draw needn't show every extreme that they name: For each source device s, the entries send_list[s, :, :] name each of its 512 prompt rows exactly once; every slot is filled. `ctx_len`: some row reaches 1024.
All inputs are finite; a program needn't handle non-finite values.
Results may differ from a plain program's by a relative error of at most 0.014.
Values may be sent and summed in bfloat16 or wider, within the bound.
A program may use at most 64 MiB of HBM per device.

v0:
```python
import jax
import jax.numpy as jnp
from jax import lax
from jax.sharding import PartitionSpec as P

score_scale = 192.0 ** (-0.5)
epsilon = 1e-06


def prefill_rows(kv_pre, kv_gain, row_start):
    values = kv_pre.astype(jnp.float32)
    lat_width = kv_gain.shape[0]
    latent = values[:, :lat_width]
    mean_square = jnp.mean(latent * latent, axis=-1, keepdims=True)
    normed = latent * lax.rsqrt(mean_square + epsilon) * kv_gain
    rotary = values[:, lat_width:]
    half_width = rotary.shape[1] // 2
    position = (row_start + jnp.arange(values.shape[0], dtype=jnp.int32)).astype(jnp.float32)
    frequency = 10000.0 ** (-jnp.arange(half_width, dtype=jnp.float32) / half_width)
    angles = position[:, None] * frequency[None, :]
    first_half = rotary[:, :half_width]
    second = rotary[:, half_width:]
    cosine = jnp.cos(angles)
    sine_part = jnp.sin(angles)
    return jnp.concatenate(
        [
            normed,
            first_half * cosine - second * sine_part,
            first_half * sine_part + second * cosine,
        ],
        axis=1,
    ).astype(jnp.bfloat16)


def attend(query, cache_rows, lengths, fresh_rows, owner_row, lat_width):
    row_count = query.shape[0]
    score_cache = (
        jnp.einsum("rhw,rkw->rhk", query, cache_rows, preferred_element_type=jnp.float32)
        * score_scale
    )
    score_fresh = (
        jnp.einsum("rhw,kw->rhk", query, fresh_rows, preferred_element_type=jnp.float32)
        * score_scale
    )
    live_cache = (
        jnp.arange(cache_rows.shape[1], dtype=jnp.int32)[None, None, :] < lengths[:, None, None]
    )
    live_fresh = owner_row[None, None, :] == jnp.arange(row_count, dtype=jnp.int32)[:, None, None]
    score_cache = jnp.where(live_cache, score_cache, -jnp.inf)
    score_fresh = jnp.where(live_fresh, score_fresh, -jnp.inf)
    peak = jnp.maximum(
        jnp.max(score_cache, axis=-1, keepdims=True), jnp.max(score_fresh, axis=-1, keepdims=True)
    )
    weight_cache = jnp.exp(score_cache - peak)
    weight_fresh = jnp.exp(score_fresh - peak)
    denominator = jnp.sum(weight_cache, axis=-1, keepdims=True) + jnp.sum(
        weight_fresh, axis=-1, keepdims=True
    )
    prob_cache = (weight_cache / denominator).astype(jnp.bfloat16)
    prob_fresh = (weight_fresh / denominator).astype(jnp.bfloat16)
    summed = jnp.einsum(
        "rhk,rkl->rhl", prob_cache, cache_rows[..., :lat_width], preferred_element_type=jnp.float32
    )
    summed = summed + jnp.einsum(
        "rhk,kl->rhl", prob_fresh, fresh_rows[:, :lat_width], preferred_element_type=jnp.float32
    )
    return summed.astype(jnp.bfloat16)


def body(kv_pre, kv_gain, send_list, row_owner, queries, cache, ctx_len, value_up):
    pool_count = lax.axis_size("pool")
    ep_count = lax.axis_size("ep")
    prompt_rows = kv_pre.shape[0]
    lat_width = kv_gain.shape[0]
    row_start = lax.axis_index(("pool", "ep")) * prompt_rows
    latent_rows = prefill_rows(kv_pre, kv_gain, row_start)
    row_width = latent_rows.shape[1]
    send_slots = send_list[0]
    capacity = send_slots.shape[1]
    filled = send_slots >= 0
    picked = jnp.maximum(send_slots, 0)
    outgoing = jnp.where(filled[:, :, None], latent_rows[picked], jnp.zeros((), jnp.bfloat16))
    outgoing = outgoing.reshape(pool_count, ep_count, capacity, row_width)
    owner_tags = jnp.where(filled, row_owner[picked] + 1, 0).astype(jnp.bfloat16)
    owner_tags = owner_tags.reshape(pool_count, ep_count, capacity)
    arrived, labels = (
        lax.all_to_all(
            lax.all_to_all(outgoing, "pool", split_axis=0, concat_axis=0, tiled=True),
            "ep",
            split_axis=1,
            concat_axis=1,
            tiled=True,
        ),
        lax.all_to_all(
            lax.all_to_all(owner_tags, "pool", split_axis=0, concat_axis=0, tiled=True),
            "ep",
            split_axis=1,
            concat_axis=1,
            tiled=True,
        ),
    )
    fresh_rows = arrived.reshape(-1, row_width)
    owner_row = labels.reshape(-1).astype(jnp.int32) - 1
    attended = attend(queries, cache, ctx_len, fresh_rows, owner_row, lat_width)
    row_count = attended.shape[0]
    head_local = value_up.shape[0]
    blocks = attended.reshape(row_count, ep_count, head_local, lat_width)
    gathered = lax.all_to_all(blocks, "ep", split_axis=1, concat_axis=0, tiled=True)
    projected = jnp.einsum(
        "rxhl,hlv->rxhv", gathered, value_up, preferred_element_type=jnp.float32
    ).astype(jnp.bfloat16)
    returned = lax.all_to_all(projected, "ep", split_axis=0, concat_axis=1, tiled=True)
    return returned.reshape(row_count, ep_count * head_local, value_up.shape[2])


def solution(mesh):
    in_specs = (
        P(("pool", "ep"), None),
        P(),
        P(("pool", "ep"), None, None),
        P(("pool", "ep")),
        P(("pool", "ep"), None, None),
        P(("pool", "ep"), None, None),
        P(("pool", "ep")),
        P("ep", None, None),
    )
    out_specs = P(("pool", "ep"), None, None)
    return jax.shard_map(body, mesh=mesh, in_specs=in_specs, out_specs=out_specs, check_vma=False)
```

profile of v0, /device:TPU:1, one launch (start us, length us, event | category | flops | bytes accessed | tf_op | source)
XLA Modules:
  0.0 131.1 jit_solution(13693426046038760260)
XLA Ops:
  0.0 0.0 copy-start
  0.0 0.0 copy-start.5
  0.0 0.0 copy-start.1
  0.0 0.0 copy-start.3
  0.0 0.8 broadcast_maximum_fusion
  0.8 0.0 copy-done.1
  0.8 3.5 %gather_fusion = s32[512]{0:T(512)S(1)} fusion(s32[512]{0:T(512)S(1)} %copy-done.1, s32[1024]{0:T(1024)S(1)} %pad_clamp_fusion), kind=kCustom, calls=%fused_computation | custom fusion | bytes 6144 | tf_op jit(solution)/shard_map/gather | solution.py:84
  4.3 0.0 copy-done.5
  4.3 0.6 fusion.31
  4.9 4.8 %all-to-all-start = ((bf16[4,128,1]{1,2,0:T(2,128)(2,1)}), bf16[4,128,1]{1,2,0:T(2,128)(2,1)S(1)}, u32[]{:S(2)}, u32[]{:S(2)}) async-start(bf16[4,128,1]{1,2,0:T(2,128)(2,1)} %fusion.31), calls=%async_computation | async-start | bytes 4096 | tf_op jit(solution)/shard_map/all_to_all | solution.py:95
  9.8 0.0 copy-done.3
  9.8 0.0 copy-start.6
  9.8 0.1 convert_element_type.54
  10.0 0.1 multiply_reduce_fusion
  10.1 0.3 fusion.28
  10.4 0.1 copy-done.6
  10.5 0.1 multiply_convert_fusion
  10.7 0.3 copy.59
  11.0 2.0 %gather_fusion.1 = bf16[512,576]{1,0:T(8,128)(2,1)S(1)} fusion(bf16[512,576]{1,0:T(8,128)(2,1)S(1)} %copy.59, s32[1024]{0:T(1024)S(1)} %pad_clamp_fusion), kind=kCustom, calls=%fused_computation.1 | custom fusion | bytes 1181696 | tf_op jit(solution)/shard_map/gather | solution.py:82
  13.0 0.3 copy.60
  13.3 0.9 broadcast_select_fusion
  14.2 0.0 all-to-all-done
  14.2 4.2 %all-to-all-start.2 = ((bf16[4,128,1,576]{1,3,2,0:T(8,128)(2,1)}), bf16[4,128,1,576]{1,3,2,0:T(8,128)(2,1)S(1)}, u32[]{:S(2)}, u32[]{:S(2)}) async-start(bf16[4,128,1,576]{1,3,2,0:T(8,128)(2,1)} %broadcast_select_fusion), calls=%async_computation.2 | async-start | bytes 1179648 | tf_op jit(solution)/shard_map/all_to_all | solution.py:88
  18.4 0.8 copy.57
  19.2 6.5 %all-to-all-done.2 = bf16[4,128,1,576]{1,3,2,0:T(8,128)(2,1)S(1)} async-done(((bf16[4,128,1,576]{1,3,2,0:T(8,128)(2,1)}), bf16[4,128,1,576]{1,3,2,0:T(8,128)(2,1)S(1)}, u32[]{:S(2)}, u32[]{:S(2)}) %all-to-all-start.2) | async-done | bytes 589856 | tf_op jit(solution)/shard_map/all_to_all | solution.py:88
  25.7 20.8 %all-to-all-start.1 = ((bf16[4,128,1]{0,2,1:T(2,128)(2,1)}), bf16[4,128,1]{0,2,1:T(2,128)(2,1)S(1)}, u32[]{:S(2)}, u32[]{:S(2)}) async-start(bf16[4,128,1]{0,2,1:T(2,128)(2,1)} %copy.57), calls=%async_computation.1 | async-start | bytes 131072 | tf_op jit(solution)/shard_map/all_to_all | solution.py:94
  46.5 0.0 copy-start.7
  46.5 1.3 %copy.61 = bf16[4,128,1,576]{3,0,2,1:T(4,128)(2,1)} copy(bf16[4,128,1,576]{1,3,2,0:T(8,128)(2,1)S(1)} %all-to-all-done.2) | data formatting | bytes 1179648 | tf_op jit(solution)/shard_map/all_to_all | solution.py:88
  47.8 10.1 %all-to-all-done.1 = bf16[4,128,1]{0,2,1:T(2,128)(2,1)S(1)} async-done(((bf16[4,128,1]{0,2,1:T(2,128)(2,1)}), bf16[4,128,1]{0,2,1:T(2,128)(2,1)S(1)}, u32[]{:S(2)}, u32[]{:S(2)}) %all-to-all-start.1) | async-done | bytes 1056 | tf_op jit(solution)/shard_map/all_to_all | solution.py:94
  57.9 5.7 %all-to-all-start.3 = ((bf16[4,128,1,576]{3,0,2,1:T(4,128)(2,1)}), bf16[4,128,1,576]{3,0,2,1:T(4,128)(2,1)S(1)}, u32[]{:S(2)}, u32[]{:S(2)}) async-start(bf16[4,128,1,576]{3,0,2,1:T(4,128)(2,1)} %copy.61), calls=%async_computation.3 | async-start | bytes 1310720 | tf_op jit(solution)/shard_map/all_to_all | solution.py:87
  63.7 0.0 copy-done.7
  63.7 0.1 iota_compare_fusion
  63.8 0.0 copy-done
  63.8 2.4 %fusion.32 = (f32[2,128]{1,0:T(2,128)S(1)}, f32[2,128,1024]{2,1,0:T(8,128)S(1)}) fusion(bf16[2,128,576]{1,2,0:T(8,128)(2,1)S(1)} %copy-done, bf16[2,1024,576]{1,2,0:T(8,128)(2,1)} %param.13, pred[2,1024]{1,0:T(4,128)(4,1)S(1)} %iota_compare_fusion), kind=kOutput, calls=%fused_computation.54 | convolution fusion | flops 302776064 | bytes 3705856 | tf_op jit(solution)/shard_map/rhw,rkw->rhk/dot_general | solution.py:38
  66.2 0.1 copy.58
  66.3 19.8 %all-to-all-done.3 = bf16[4,128,1,576]{3,0,2,1:T(4,128)(2,1)S(1)} async-done(((bf16[4,128,1,576]{3,0,2,1:T(4,128)(2,1)}), bf16[4,128,1,576]{3,0,2,1:T(4,128)(2,1)S(1)}, u32[]{:S(2)}, u32[]{:S(2)}) %all-to-all-start.3) | async-done | bytes 589856 | tf_op jit(solution)/shard_map/all_to_all | solution.py:87
  86.1 0.9 copy.62
  87.0 0.2 reshape.215
  87.3 0.1 copy.77
  87.4 0.4 fusion.33
  87.8 0.3 fusion.15
  88.1 0.1 fusion.19
  88.2 0.0 copy-start.2
  88.2 0.4 fusion.16
  88.6 1.3 copy-done.2
  89.9 0.9 fusion.11
  90.8 0.0 copy-start.4
  90.8 0.3 copy.66
  91.0 21.0 %all_to_all.50 = bf16[2,128,1,512]{3,0,2,1:T(2,128)(2,1)S(1)} all-to-all(bf16[2,128,1,512]{3,0,2,1:T(2,128)(2,1)S(1)} %copy.66), channel_id=1, replica_groups=mesh['pool'=4,'ep'=128] {'ep'}, dimensions={1} | all-to-all | bytes 524288 | tf_op jit(solution)/shard_map/all_to_all | solution.py:108
  112.0 0.1 reshape.190
  112.1 0.0 copy-done.4
  112.1 0.2 fusion.14
  112.4 0.1 copy.78
  112.5 17.9 %all_to_all.51 = bf16[128,2,128]{2,1,0:T(2,128)(2,1)S(1)} all-to-all(bf16[128,2,128]{2,1,0:T(2,128)(2,1)S(1)} %bitcast.63), channel_id=1, replica_groups=mesh['pool'=4,'ep'=128] {'ep'}, dimensions={0} | all-to-all | bytes 131072 | tf_op jit(solution)/shard_map/all_to_all | solution.py:112
  130.4 0.6 copy.68
  (14 shorter events, 0.2 us)
Async XLA Ops:
  0.0 63.8 %copy-start = (bf16[2,128,576]{1,2,0:T(8,128)(2,1)S(1)}, bf16[2,128,576]{1,2,0:T(8,128)(2,1)}, u32[]{:S(2)}) copy-start(bf16[2,128,576]{1,2,0:T(8,128)(2,1)} %param.12) | copy-start | bytes 884740
  0.0 4.3 %copy-start.5 = (s32[1,512,1]{1,2,0:T(1,128)S(1)}, s32[1,512,1]{1,2,0:T(1,128)}, u32[]{:S(2)}) copy-start(s32[1,512,1]{1,2,0:T(1,128)} %param.10) | copy-start | bytes 6148
  0.0 0.8 copy-start.1
  0.0 9.8 %copy-start.3 = (bf16[512,576]{0,1:T(8,128)(2,1)S(1)}, bf16[512,576]{0,1:T(8,128)(2,1)}, u32[]{:S(2)}) copy-start(bf16[512,576]{0,1:T(8,128)(2,1)} %param.8) | copy-start | bytes 1769476
  4.9 9.3 %all-to-all-start = ((bf16[4,128,1]{1,2,0:T(2,128)(2,1)}), bf16[4,128,1]{1,2,0:T(2,128)(2,1)S(1)}, u32[]{:S(2)}, u32[]{:S(2)}) async-start(bf16[4,128,1]{1,2,0:T(2,128)(2,1)} %fusion.31), calls=%async_computation | async-start | bytes 4096 | tf_op jit(solution)/shard_map/all_to_all | solution.py:95
  9.8 0.7 copy-start.6
  14.2 11.5 %all-to-all-start.2 = ((bf16[4,128,1,576]{1,3,2,0:T(8,128)(2,1)}), bf16[4,128,1,576]{1,3,2,0:T(8,128)(2,1)S(1)}, u32[]{:S(2)}, u32[]{:S(2)}) async-start(bf16[4,128,1,576]{1,3,2,0:T(8,128)(2,1)} %broadcast_select_fusion), calls=%async_computation.2 | async-start | bytes 1179648 | tf_op jit(solution)/shard_map/all_to_all | solution.py:88
  25.7 32.2 %all-to-all-start.1 = ((bf16[4,128,1]{0,2,1:T(2,128)(2,1)}), bf16[4,128,1]{0,2,1:T(2,128)(2,1)S(1)}, u32[]{:S(2)}, u32[]{:S(2)}) async-start(bf16[4,128,1]{0,2,1:T(2,128)(2,1)} %copy.57), calls=%async_computation.1 | async-start | bytes 131072 | tf_op jit(solution)/shard_map/all_to_all | solution.py:94
  46.5 17.2 %copy-start.7 = (s32[2]{0:T(128)S(1)}, s32[2]{0:T(128)}, u32[]{:S(2)}) copy-start(s32[2]{0:T(128)} %param.14) | copy-start | bytes 28
  57.9 28.2 %all-to-all-start.3 = ((bf16[4,128,1,576]{3,0,2,1:T(4,128)(2,1)}), bf16[4,128,1,576]{3,0,2,1:T(4,128)(2,1)S(1)}, u32[]{:S(2)}, u32[]{:S(2)}) async-start(bf16[4,128,1,576]{3,0,2,1:T(4,128)(2,1)} %copy.61), calls=%async_computation.3 | async-start | bytes 1310720 | tf_op jit(solution)/shard_map/all_to_all | solution.py:87
  88.2 1.7 %copy-start.2 = (bf16[2,1024,576]{1,2,0:T(8,128)(2,1)S(1)}, bf16[2,1024,576]{1,2,0:T(8,128)(2,1)}, u32[]{:S(2)}) copy-start(bf16[2,1024,576]{1,2,0:T(8,128)(2,1)} %param.13) | copy-start | bytes 7077892
  90.8 21.4 %copy-start.4 = (bf16[1,512,128]{2,1,0:T(8,128)(2,1)S(1)}, bf16[1,512,128]{2,1,0:T(8,128)(2,1)}, u32[]{:S(2)}) copy-start(bf16[1,512,128]{2,1,0:T(8,128)(2,1)} %param.15) | copy-start | bytes 393220
where the time goes:
time: 132 us; the launch traced here: 131 us
  blocking collectives  38.9 us (29%)
  waiting for transfers between devices  36.4 us (28%)
  starting transfers between devices  35.6 us (27%)
  local copies, waits for them, and re-layouts  12.1 us (9%)
  matrix products  4.29 us (3%)
  other arithmetic  3.53 us (3%)
    all_to_all x1, blocking collectives, body(): lax.all_to_all(blocks, 'ep', split_axis=1, concat_axis=0, tiled=True)  21 us
    all_to_all x1, starting transfers between devices, body(): lax.all_to_all(lax.all_to_all(owner_tags, 'pool', split_axis=0, concat_ax...  20.8 us
    all_to_all x1, waiting for transfers between devices, body(): lax.all_to_all(lax.all_to_all(outgoing, 'pool', split_axis=0, concat_axis...  19.8 us
    all_to_all x1, blocking collectives, body(): lax.all_to_all(projected, 'ep', split_axis=0, concat_axis=1, tiled=True)  17.9 us
    all_to_all x1, waiting for transfers between devices, body(): lax.all_to_all(lax.all_to_all(owner_tags, 'pool', split_axis=0, concat_ax...  10.1 us
    all_to_all x1, waiting for transfers between devices, body(): lax.all_to_all(outgoing, 'pool', split_axis=0, concat_axis=0, tiled=True)  6.51 us
    all_to_all x1, starting transfers between devices, body(): lax.all_to_all(lax.all_to_all(outgoing, 'pool', split_axis=0, concat_axis...  5.73 us
    all_to_all x1, starting transfers between devices, body(): lax.all_to_all(owner_tags, 'pool', split_axis=0, concat_axis=0, tiled=True)  4.84 us
  transfers between devices with their start and end apart: 4, of which 3 were waited for; matrix products, arithmetic and copies ran while one was open for 7% of the time, Pallas kernels for 0%

commit v1 on v0

v1 whole, which is shorter than its diff:
```python
import functools
import math

import jax
import jax.numpy as jnp
import numpy as np
from jax import lax
from jax.experimental import pallas as pl
from jax.experimental.pallas import tpu as pltpu
from jax.sharding import PartitionSpec as P

MESH = pl.DeviceIdType.MESH
score_scale = 192.0 ** (-0.5)
epsilon = 1e-06
f32 = jnp.float32
bf16 = jnp.bfloat16
masked = -1e30


def far_first(step, size):
    return size // 2 + ((step + 1) // 2) * (1 - 2 * (step % 2))


def dot_nn(a, b):
    return jnp.dot(a, b, preferred_element_type=f32)


def dot_nt(a, b):
    return lax.dot_general(a, b, (((1,), (1,)), ((), ())), preferred_element_type=f32)


def iota(shape, dim):
    return lax.broadcasted_iota(jnp.int32, shape, dim)


def one_hot(condition):
    return jnp.where(condition, 1.0, 0.0).astype(bf16)


def kernel(
    nx, ny, nz, lat, rope,
    freq_ref, gain_ref, send_ref, owner_ref, len_ref,
    kv_hbm, query_hbm, cache_hbm, value_hbm,
    out_ref,
    kv, query_t, cache, value, qpad, core_out, core_in,
    msg1, got1, msg2, got2, msg3, got3,
    load_sem, core_send, core_recv, val_send, val_recv,
    send1, recv1, send2, recv2, send3, recv3, plane_sem,
):
    x = lax.axis_index("pool")
    ep = lax.axis_index("ep")
    y = ep // (2 * nz)
    z = (ep % (2 * nz)) // 2
    core = ep % 2
    chip = (x * ny + y) * nz + z
    place = y * nz + z
    chips = nx * ny * nz
    places = ny * nz
    prompt = kv.shape[1]
    width = lat + rope
    padded = kv.shape[0]
    heads = query_t.shape[2]
    half = rope // 2
    partner = (x, ep + 1 - 2 * core)

    def device(cx, cy, cz):
        return (cx, (cy * nz + cz) * 2 + core)

    barrier = pltpu.get_barrier_semaphore()

    def greet_plane(step, carry):
        cx = (x + step // ny) % nx
        cy = (y + step % ny) % ny
        pl.semaphore_signal(barrier, inc=1, device_id=device(cx, cy, z), device_id_type=MESH)
        return carry

    def greet_ring(step, carry):
        pl.semaphore_signal(
            barrier, inc=1, device_id=device(x, y, (z + step) % nz), device_id_type=MESH
        )
        return carry

    lax.fori_loop(1, nx * ny, greet_plane, 0)
    lax.fori_loop(1, nz, greet_ring, 0)
    pl.semaphore_signal(barrier, inc=1, device_id=partner, device_id_type=MESH)

    load_kv = pltpu.make_async_copy(kv_hbm, kv.at[pl.ds(0, width)], load_sem.at[0])
    load_value = pltpu.make_async_copy(value_hbm.at[0], value.at[core], load_sem.at[1])
    load_query = pltpu.make_async_copy(query_hbm, query_t, load_sem.at[2])
    load_cache = pltpu.make_async_copy(cache_hbm, cache, load_sem.at[3])
    load_kv.start()
    load_value.start()
    load_query.start()
    load_cache.start()

    send_row = send_ref[...].astype(f32)
    lane = iota((chips, prompt), 1)
    line = iota((chips, prompt), 0)
    send_other = jnp.sum(
        jnp.where(lane == 2 * line + (1 - core), send_row, 0.0), axis=1, keepdims=True
    )
    wide_lane = iota((2 * chips, prompt), 1)
    wide_line = iota((2 * chips, prompt), 0)
    send_own = jnp.sum(jnp.where(wide_lane == wide_line, send_row, 0.0), axis=1, keepdims=True)
    pick_other = one_hot(lane.astype(f32) == send_other)
    pick_own = one_hot(
        jnp.logical_and(wide_lane.astype(f32) == send_own, wide_line % 2 == core)
    )

    first_row = ((x * ny + y) * nz + z) * 2 + core
    position = (first_row * prompt + iota((half, prompt), 1)).astype(f32)
    angles = position * freq_ref[...]
    turns = jnp.floor(angles * (1.0 / (2.0 * math.pi)) + 0.5)
    angles = ((angles - turns * 6.28125) - turns * 0.0019340515136718750) - turns * 1.2556659146e-06
    cosine = jnp.cos(angles)
    sine = jnp.sin(angles)
    load_kv.wait()
    first = kv[lat : lat + half, :].astype(f32)
    second = kv[lat + half : width, :].astype(f32)
    kv[lat : lat + half, :] = (first * cosine - second * sine).astype(bf16)
    kv[lat + half : width, :] = (first * sine + second * cosine).astype(bf16)
    tail = padded - width
    kv[width:padded, :] = jnp.where(
        iota((tail, prompt), 0) == 0, owner_ref[...].astype(f32), 0.0
    ).astype(bf16)

    def rows_of(pick):
        picked = dot_nt(pick, kv[...])
        latent = picked[:, :lat]
        mean_square = jnp.mean(latent * latent, axis=1, keepdims=True)
        normed = latent * lax.rsqrt(mean_square + epsilon) * gain_ref[...]
        return jnp.concatenate([normed, picked[:, lat:]], axis=1).astype(bf16)

    core_out[...] = rows_of(pick_other)

    pl.semaphore_wait(barrier, nx * ny - 1 + nz - 1 + 1)

    def plane_ready(step, carry):
        pl.semaphore_signal(
            plane_sem, inc=1, device_id=device(x, y, (z + step) % nz), device_id_type=MESH
        )
        return carry

    lax.fori_loop(1, nz, plane_ready, 0)
    swap = pltpu.make_async_remote_copy(
        src_ref=core_out, dst_ref=core_in, send_sem=core_send, recv_sem=core_recv,
        device_id=partner, device_id_type=MESH,
    )
    swap.start()
    load_value.wait()
    swap_value = pltpu.make_async_remote_copy(
        src_ref=value.at[core], dst_ref=value.at[core], send_sem=val_send, recv_sem=val_recv,
        device_id=partner, device_id_type=MESH,
    )
    swap_value.start()

    own_rows = rows_of(pick_own)
    spread = one_hot(iota((2 * chips, chips), 0) == 2 * iota((2 * chips, chips), 1) + (1 - core))
    swap.wait()
    both = own_rows.astype(f32) + dot_nn(spread, core_in[...])
    msg1[...] = both.astype(bf16).reshape(chips, 2, padded)

    pl.semaphore_wait(plane_sem, nz - 1)

    def send_rows(step, carry):
        cx = (x + far_first(step // places, nx)) % nx
        cy = (y + far_first((step // nz) % ny, ny)) % ny
        cz = (z + far_first(step % nz, nz)) % nz
        pltpu.make_async_remote_copy(
            src_ref=msg1.at[(cx * ny + cy) * nz + cz], dst_ref=got1.at[chip],
            send_sem=send1, recv_sem=recv1, device_id=device(cx, cy, cz), device_id_type=MESH,
        ).start()
        return carry

    lax.fori_loop(0, chips - 1, send_rows, 0)
    got1[pl.ds(chip, 1)] = msg1[pl.ds(chip, 1)]

    load_query.wait()
    unit = one_hot(iota((heads, heads), 0) == iota((heads, heads), 1))
    for r in range(2):
        qpad[r * heads : (r + 1) * heads, :] = jnp.concatenate(
            [dot_nt(unit, query_t[r]), jnp.zeros((heads, tail), f32)], axis=1
        ).astype(bf16)
    qpad[2 * heads : 2 * heads + 16, :] = one_hot(
        jnp.logical_and(iota((16, padded), 0) == 0, iota((16, padded), 1) == width)
    )

    load_cache.wait()
    peaks, sums, totals = [], [], []
    for r in range(2):
        scores = dot_nn(qpad[r * heads : (r + 1) * heads, :width], cache[r]) * score_scale
        scores = jnp.where(iota(scores.shape, 1) < len_ref[r], scores, masked)
        peak = jnp.max(scores, axis=1, keepdims=True)
        weight = jnp.exp(scores - peak)
        peaks.append(peak)
        sums.append(jnp.sum(weight, axis=1, keepdims=True))
        totals.append(dot_nt(weight.astype(bf16), cache[r, :lat, :]))
    peak_cache = jnp.concatenate(peaks, axis=0)
    sum_cache = jnp.concatenate(sums, axis=0)
    total_cache = jnp.concatenate(totals, axis=0)

    all_rows = pltpu.make_async_copy(
        msg1.at[pl.ds(0, chips - 1)], got1.at[pl.ds(0, chips - 1)], recv1
    )
    all_rows.wait()
    fresh = got1[...].reshape(2 * chips, padded)
    raw = dot_nt(qpad[...], fresh)
    owner = raw[2 * heads : 2 * heads + 1, :]
    scores = raw[: 2 * heads, :] * score_scale
    row = (iota(scores.shape, 0) // heads).astype(f32)
    scores = jnp.where(row == owner, scores, masked)
    peak = jnp.maximum(peak_cache, jnp.max(scores, axis=1, keepdims=True))
    weight = jnp.exp(scores - peak)
    scale_cache = jnp.exp(peak_cache - peak)
    denominator = sum_cache * scale_cache + jnp.sum(weight, axis=1, keepdims=True)
    total = total_cache * scale_cache + dot_nn(weight.astype(bf16), fresh[:, :lat])
    attended = (total / denominator).astype(bf16)

    line = iota((2 * heads, 2 * heads), 0)
    lane = iota((2 * heads, 2 * heads), 1)
    by_chip = one_hot(lane == ((line // 2) % 2) * heads + (line // 4) * 2 + line % 2)
    msg2[...] = dot_nn(by_chip, attended).astype(bf16).reshape(places, 4, lat)

    def send_heads(step, carry):
        cy = (y + far_first(step // nz, ny)) % ny
        cz = (z + far_first(step % nz, nz)) % nz
        pltpu.make_async_remote_copy(
            src_ref=msg2.at[cy * nz + cz], dst_ref=got2.at[place],
            send_sem=send2, recv_sem=recv2, device_id=device(x, cy, cz), device_id_type=MESH,
        ).start()
        return carry

    lax.fori_loop(0, places - 1, send_heads, 0)
    got2[pl.ds(place, 1)] = msg2[pl.ds(place, 1)]
    swap_value.wait()
    weights = jnp.concatenate([value[0], value[1]], axis=1)
    pltpu.make_async_copy(
        msg2.at[pl.ds(0, places - 1)], got2.at[pl.ds(0, places - 1)], recv2
    ).wait()
    vhead = value.shape[2]
    projected = dot_nn(got2[...].reshape(4 * places, lat), weights)
    even = iota((4 * places, vhead), 0) % 2 == 0
    mine = jnp.where(even, projected[:, :vhead], projected[:, vhead:])
    msg3[...] = mine.astype(bf16).reshape(places, 4, vhead)

    def send_back(step, carry):
        cy = (y + far_first(step // nz, ny)) % ny
        cz = (z + far_first(step % nz, nz)) % nz
        pltpu.make_async_remote_copy(
            src_ref=msg3.at[cy * nz + cz], dst_ref=got3.at[place],
            send_sem=send3, recv_sem=recv3, device_id=device(x, cy, cz), device_id_type=MESH,
        ).start()
        return carry

    lax.fori_loop(0, places - 1, send_back, 0)
    got3[pl.ds(place, 1)] = msg3[pl.ds(place, 1)]
    by_row = one_hot(line == ((lane // 2) % 2) * heads + (lane // 4) * 2 + lane % 2)
    pltpu.make_async_copy(
        msg3.at[pl.ds(0, places - 1)], got3.at[pl.ds(0, places - 1)], recv3
    ).wait()
    out_ref[...] = (
        dot_nn(by_row, got3[...].reshape(4 * places, vhead)).astype(bf16).reshape(2, heads, vhead)
    )

    pltpu.make_async_copy(
        msg1.at[pl.ds(0, chips - 1)], got1.at[pl.ds(0, chips - 1)], send1
    ).wait()
    pltpu.make_async_copy(
        msg2.at[pl.ds(0, places - 1)], got2.at[pl.ds(0, places - 1)], send2
    ).wait()
    pltpu.make_async_copy(
        msg3.at[pl.ds(0, places - 1)], got3.at[pl.ds(0, places - 1)], send3
    ).wait()


def body(kv_pre, kv_gain, send_list, row_owner, queries, cache, ctx_len, value_up):
    nx = lax.axis_size("pool")
    places = lax.axis_size("ep") // 2
    ny = nz = math.isqrt(places)
    chips = nx * places
    lat = kv_gain.shape[0]
    width = kv_pre.shape[1]
    rope = width - lat
    prompt = kv_pre.shape[0]
    rows, heads, _ = queries.shape
    slots = cache.shape[1]
    vhead = value_up.shape[2]
    padded = -(-(width + 1) // 128) * 128
    half = rope // 2
    frequency = np.float32(10000.0) ** (-np.arange(half, dtype=np.float32) / np.float32(half))
    frequency = np.broadcast_to(frequency.astype(np.float32)[:, None], (half, prompt))

    vmem = pl.BlockSpec(memory_space=pltpu.VMEM)
    smem = pl.BlockSpec(memory_space=pltpu.SMEM)
    hbm = pl.BlockSpec(memory_space=pl.ANY)
    dma = pltpu.SemaphoreType.DMA
    return pl.pallas_call(
        functools.partial(kernel, nx, ny, nz, lat, rope),
        out_shape=jax.ShapeDtypeStruct((rows, heads, vhead), bf16),
        in_specs=[vmem, vmem, vmem, vmem, smem, hbm, hbm, hbm, hbm],
        out_specs=vmem,
        scratch_shapes=[
            pltpu.VMEM((padded, prompt), bf16),
            pltpu.VMEM((rows, width, heads), bf16),
            pltpu.VMEM((rows, width, slots), bf16),
            pltpu.VMEM((2, lat, vhead), bf16),
            pltpu.VMEM((rows * heads + 16, padded), bf16),
            pltpu.VMEM((chips, padded), bf16),
            pltpu.VMEM((chips, padded), bf16),
            pltpu.VMEM((chips, 2, padded), bf16),
            pltpu.VMEM((chips, 2, padded), bf16),
            pltpu.VMEM((places, 4, lat), bf16),
            pltpu.VMEM((places, 4, lat), bf16),
            pltpu.VMEM((places, 4, vhead), bf16),
            pltpu.VMEM((places, 4, vhead), bf16),
            dma((4,)),
            dma, dma, dma, dma,
            dma, dma, dma, dma, dma, dma,
            pltpu.SemaphoreType.REGULAR,
        ],
        compiler_params=pltpu.CompilerParams(
            collective_id=0, has_side_effects=True, vmem_limit_bytes=56 * 2**20
        ),
        name="serve_window",
    )(
        jnp.asarray(frequency),
        kv_gain.reshape(1, lat),
        send_list.reshape(1, prompt),
        row_owner.reshape(1, prompt),
        ctx_len,
        kv_pre.T,
        queries.transpose(0, 2, 1),
        cache.transpose(0, 2, 1),
        value_up,
    )


def solution(mesh):
    in_specs = (
        P(("pool", "ep"), None),
        P(),
        P(("pool", "ep"), None, None),
        P(("pool", "ep")),
        P(("pool", "ep"), None, None),
        P(("pool", "ep"), None, None),
        P(("pool", "ep")),
        P("ep", None, None),
    )
    out_specs = P(("pool", "ep"), None, None)
    return jax.shard_map(body, mesh=mesh, in_specs=in_specs, out_specs=out_specs, check_vma=False)
```

time: 132 us -> 62.1 us (0.47)
  Pallas kernels: 0 us -> 59.1 us
  blocking collectives: 38.9 us -> 0 us
  waiting for transfers between devices: 36.4 us -> 0 us
  starting transfers between devices: 35.6 us -> 0 us
  local copies, waits for them, and re-layouts: 12.1 us -> 2.83 us
  matrix products: 4.29 us -> 0 us
  other arithmetic: 3.53 us -> 0 us
    pallas_call x0 -> x1, Pallas kernels: none -> 59.1 us  [body(): pl.pallas_call(functools.partial(kernel, nx, ny, nz, lat, rope), out_shap...]
    all_to_all x2 -> x0, blocking collectives: 38.9 us -> none  [the longest x1 21 us: body(): lax.all_to_all(blocks, 'ep', split_axis=1, concat_axis=0, tiled=True)]
    all_to_all x4 -> x0, waiting for transfers between devices: 36.4 us -> none  [the longest x1 19.8 us: body(): lax.all_to_all(lax.all_to_all(outgoing, 'pool', split_axis=0, concat_axis...]
    all_to_all x4 -> x0, starting transfers between devices: 35.6 us -> none  [the longest x1 20.8 us: body(): lax.all_to_all(lax.all_to_all(owner_tags, 'pool', split_axis=0, concat_ax...]
    gather x3 -> x0, local copies, waits for them, and re-layouts: 5.83 us -> none  [the longest x1 3.49 us: body(): row_owner[picked] + 1]
    dot_general x5 -> x0, matrix products: 4.29 us -> none  [the longest x1 2.43 us: attend(): jnp.einsum('rhw,rkw->rhk', query, cache_rows, preferred_element_type=jnp....]
    all_to_all x4 -> x0, local copies, waits for them, and re-layouts: 3.14 us -> none  [the longest x1 1.35 us: body(): lax.all_to_all(outgoing, 'pool', split_axis=0, concat_axis=0, tiled=True)]
  transfers between devices with their start and end apart: 4 -> 0, of which waited for: 3 -> 0; matrix products, arithmetic and copies ran while one was open for 7% -> 0% of each run, Pallas kernels for 0% -> 0%
where the time goes in v1:
time: 62.1 us; the launch traced here: 61.9 us
  Pallas kernels  59.1 us (95%)
  local copies, waits for them, and re-layouts  2.83 us (5%)
    pallas_call x1, Pallas kernels, body(): pl.pallas_call(functools.partial(kernel, nx, ny, nz, lat, rope), out_shap...  59.1 us
    unnamed x1, local copies, waits for them, and re-layouts  1.47 us
    another operation x1, local copies, waits for them, and re-layouts  1.36 us

profile of v1, /device:TPU:1, one launch (start us, length us, event | category | flops | bytes accessed | tf_op | source)
XLA Modules:
  0.0 61.9 jit_solution(6931892620629905760)
XLA Ops:
  0.0 1.4 %jit_solution_.3.freq_ref = f32[32,512]{1,0:T(8,128)} broadcast(f32[32]{0:T(128)} %constant.2.clone), dimensions={0} | broadcast | bytes 65664 | tf_op jit(solution)
  1.4 59.1 %serve_window.1 = bf16[2,128,128]{2,1,0:T(8,128)(2,1)} custom-call(f32[32,512]{1,0:T(8,128)} %jit_solution_.3.freq_ref, f32[1,512]{1,0:T(1,128)} %bitcast.9, s32[1,512]{1,0:T(1,128)} %bitcast.10, s32[1,512]{1,0:T(1,128)} %bitcast.11, s32[2]{0:T(128)} %len_ref.1, bf16[576,512]{1,0:T(8,128)(2,1)} %bitcast.7, bf16[2,576,128]{2,1,0:T(8,128)(2,1)} %bitcast.8, ...), custom_call_target="tpu_custom_call" | custom-call | tf_op jit(solution)/shard_map/serve_window/pallas_call | solution.py:297
  60.5 1.5 %copy.11 = bf16[2,128,128]{2,1,0:T(8,128)(2,1)} copy(bf16[2,128,128]{2,1,0:T(8,128)(2,1)} %serve_window.1) | data formatting | bytes 131072

commit v2 on v1

--- a/solution.py
+++ b/solution.py
@@ -18,7 +18,14 @@
 
 
 def far_first(step, size):
-    return size // 2 + ((step + 1) // 2) * (1 - 2 * (step % 2))
+    if isinstance(step, int):
+        return size // 2 + ((step + 1) // 2) * (1 - 2 * (step % 2))
+    return size // 2 + lax.div(step + 1, 2) * (1 - 2 * lax.rem(step, 2))
+
+
+def moved(position, step, size):
+    place = position + far_first(step, size)
+    return jnp.where(place >= size, place - size, place)
 
 
 def dot_nn(a, b):
@@ -39,19 +46,18 @@
 
 def kernel(
     nx, ny, nz, lat, rope,
-    freq_ref, gain_ref, send_ref, owner_ref, len_ref,
-    kv_hbm, query_hbm, cache_hbm, value_hbm,
+    gain_hbm, send_hbm, owner_hbm, len_hbm, kv_hbm, query_hbm, cache_hbm, value_hbm,
     out_ref,
-    kv, query_t, cache, value, qpad, core_out, core_in,
+    gain_ref, send_ref, owner_ref, len_ref, kv, query_t, cache, value, qpad, core_out, core_in,
     msg1, got1, msg2, got2, msg3, got3,
     load_sem, core_send, core_recv, val_send, val_recv,
     send1, recv1, send2, recv2, send3, recv3, plane_sem,
 ):
     x = lax.axis_index("pool")
     ep = lax.axis_index("ep")
-    y = ep // (2 * nz)
-    z = (ep % (2 * nz)) // 2
-    core = ep % 2
+    y = lax.div(ep, 2 * nz)
+    z = lax.div(lax.rem(ep, 2 * nz), 2)
+    core = lax.rem(ep, 2)
     chip = (x * ny + y) * nz + z
     place = y * nz + z
     chips = nx * ny * nz
@@ -68,31 +74,43 @@
 
     barrier = pltpu.get_barrier_semaphore()
 
+    far_y = [moved(y, step, ny) for step in range(ny - 1)]
+    far_z = [moved(z, step, nz) for step in range(nz - 1)]
+
+    def greet(cx, cy, cz):
+        pl.semaphore_signal(barrier, inc=1, device_id=device(cx, cy, cz), device_id_type=MESH)
+
     def greet_plane(step, carry):
-        cx = (x + step // ny) % nx
-        cy = (y + step % ny) % ny
-        pl.semaphore_signal(barrier, inc=1, device_id=device(cx, cy, z), device_id_type=MESH)
+        cx = moved(x, step, nx)
+        for cy in far_y + [y]:
+            greet(cx, cy, z)
         return carry
 
-    def greet_ring(step, carry):
-        pl.semaphore_signal(
-            barrier, inc=1, device_id=device(x, y, (z + step) % nz), device_id_type=MESH
-        )
-        return carry
-
-    lax.fori_loop(1, nx * ny, greet_plane, 0)
-    lax.fori_loop(1, nz, greet_ring, 0)
+    lax.fori_loop(0, nx - 1, greet_plane, 0)
+    for cy in far_y:
+        greet(x, cy, z)
+    for cz in far_z:
+        greet(x, y, cz)
     pl.semaphore_signal(barrier, inc=1, device_id=partner, device_id_type=MESH)
 
     load_kv = pltpu.make_async_copy(kv_hbm, kv.at[pl.ds(0, width)], load_sem.at[0])
     load_value = pltpu.make_async_copy(value_hbm.at[0], value.at[core], load_sem.at[1])
     load_query = pltpu.make_async_copy(query_hbm, query_t, load_sem.at[2])
     load_cache = pltpu.make_async_copy(cache_hbm, cache, load_sem.at[3])
+    load_gain = pltpu.make_async_copy(gain_hbm, gain_ref, load_sem.at[4])
+    load_send = pltpu.make_async_copy(send_hbm, send_ref, load_sem.at[5])
+    load_owner = pltpu.make_async_copy(owner_hbm, owner_ref, load_sem.at[6])
+    load_len = pltpu.make_async_copy(len_hbm, len_ref, load_sem.at[7])
+    load_send.start()
     load_kv.start()
+    load_owner.start()
+    load_gain.start()
+    load_len.start()
     load_value.start()
     load_query.start()
     load_cache.start()
 
+    load_send.wait()
     send_row = send_ref[...].astype(f32)
     lane = iota((chips, prompt), 1)
     line = iota((chips, prompt), 0)
@@ -109,7 +127,11 @@
 
     first_row = ((x * ny + y) * nz + z) * 2 + core
     position = (first_row * prompt + iota((half, prompt), 1)).astype(f32)
-    angles = position * freq_ref[...]
+    index = iota((half, prompt), 0)
+    frequency = jnp.zeros((half, prompt), f32)
+    for j in range(half):
+        frequency = jnp.where(index == j, float(np.float32(10000.0 ** (-j / half))), frequency)
+    angles = position * frequency
     turns = jnp.floor(angles * (1.0 / (2.0 * math.pi)) + 0.5)
     angles = ((angles - turns * 6.28125) - turns * 0.0019340515136718750) - turns * 1.2556659146e-06
     cosine = jnp.cos(angles)
@@ -120,6 +142,7 @@
     kv[lat : lat + half, :] = (first * cosine - second * sine).astype(bf16)
     kv[lat + half : width, :] = (first * sine + second * cosine).astype(bf16)
     tail = padded - width
+    load_owner.wait()
     kv[width:padded, :] = jnp.where(
         iota((tail, prompt), 0) == 0, owner_ref[...].astype(f32), 0.0
     ).astype(bf16)
@@ -131,17 +154,13 @@
         normed = latent * lax.rsqrt(mean_square + epsilon) * gain_ref[...]
         return jnp.concatenate([normed, picked[:, lat:]], axis=1).astype(bf16)
 
+    load_gain.wait()
     core_out[...] = rows_of(pick_other)
 
     pl.semaphore_wait(barrier, nx * ny - 1 + nz - 1 + 1)
 
-    def plane_ready(step, carry):
-        pl.semaphore_signal(
-            plane_sem, inc=1, device_id=device(x, y, (z + step) % nz), device_id_type=MESH
-        )
-        return carry
-
-    lax.fori_loop(1, nz, plane_ready, 0)
+    for cz in far_z:
+        pl.semaphore_signal(plane_sem, inc=1, device_id=device(x, y, cz), device_id_type=MESH)
     swap = pltpu.make_async_remote_copy(
         src_ref=core_out, dst_ref=core_in, send_sem=core_send, recv_sem=core_recv,
         device_id=partner, device_id_type=MESH,
@@ -160,19 +179,36 @@
     both = own_rows.astype(f32) + dot_nn(spread, core_in[...])
     msg1[...] = both.astype(bf16).reshape(chips, 2, padded)
 
-    pl.semaphore_wait(plane_sem, nz - 1)
-
-    def send_rows(step, carry):
-        cx = (x + far_first(step // places, nx)) % nx
-        cy = (y + far_first((step // nz) % ny, ny)) % ny
-        cz = (z + far_first(step % nz, nz)) % nz
+    def send_row(cx, cy, cz):
         pltpu.make_async_remote_copy(
             src_ref=msg1.at[(cx * ny + cy) * nz + cz], dst_ref=got1.at[chip],
             send_sem=send1, recv_sem=recv1, device_id=device(cx, cy, cz), device_id_type=MESH,
         ).start()
+
+    def send_plane(step, carry):
+        cx = moved(x, step, nx)
+        for cy in far_y + [y]:
+            send_row(cx, cy, z)
         return carry
 
-    lax.fori_loop(0, chips - 1, send_rows, 0)
+    lax.fori_loop(0, nx - 1, send_plane, 0)
+    for cy in far_y:
+        send_row(x, cy, z)
+
+    pl.semaphore_wait(plane_sem, nz - 1)
+
+    def send_slab(step, carry):
+        cx = moved(x, step, nx)
+
+        def send_ring(inner, carry):
+            cy = moved(y, inner, ny)
+            for cz in far_z:
+                send_row(cx, cy, cz)
+            return carry
+
+        return lax.fori_loop(0, ny, send_ring, carry)
+
+    lax.fori_loop(0, nx, send_slab, 0)
     got1[pl.ds(chip, 1)] = msg1[pl.ds(chip, 1)]
 
     load_query.wait()
@@ -186,6 +222,7 @@
     )
 
     load_cache.wait()
+    load_len.wait()
     peaks, sums, totals = [], [], []
     for r in range(2):
         scores = dot_nn(qpad[r * heads : (r + 1) * heads, :width], cache[r]) * score_scale
@@ -221,16 +258,21 @@
     by_chip = one_hot(lane == ((line // 2) % 2) * heads + (line // 4) * 2 + line % 2)
     msg2[...] = dot_nn(by_chip, attended).astype(bf16).reshape(places, 4, lat)
 
-    def send_heads(step, carry):
-        cy = (y + far_first(step // nz, ny)) % ny
-        cz = (z + far_first(step % nz, nz)) % nz
+    def send_heads(cy, cz):
         pltpu.make_async_remote_copy(
             src_ref=msg2.at[cy * nz + cz], dst_ref=got2.at[place],
             send_sem=send2, recv_sem=recv2, device_id=device(x, cy, cz), device_id_type=MESH,
         ).start()
+
+    def send_heads_ring(step, carry):
+        cy = moved(y, step, ny)
+        for cz in far_z:
+            send_heads(cy, cz)
         return carry
 
-    lax.fori_loop(0, places - 1, send_heads, 0)
+    lax.fori_loop(0, ny, send_heads_ring, 0)
+    for cy in far_y:
+        send_heads(cy, z)
     got2[pl.ds(place, 1)] = msg2[pl.ds(place, 1)]
     swap_value.wait()
     weights = jnp.concatenate([value[0], value[1]], axis=1)
@@ -243,16 +285,21 @@
     mine = jnp.where(even, projected[:, :vhead], projected[:, vhead:])
     msg3[...] = mine.astype(bf16).reshape(places, 4, vhead)
 
-    def send_back(step, carry):
-        cy = (y + far_first(step // nz, ny)) % ny
-        cz = (z + far_first(step % nz, nz)) % nz
+    def send_back(cy, cz):
         pltpu.make_async_remote_copy(
             src_ref=msg3.at[cy * nz + cz], dst_ref=got3.at[place],
             send_sem=send3, recv_sem=recv3, device_id=device(x, cy, cz), device_id_type=MESH,
         ).start()
+
+    def send_back_ring(step, carry):
+        cy = moved(y, step, ny)
+        for cz in far_z:
+            send_back(cy, cz)
         return carry
 
-    lax.fori_loop(0, places - 1, send_back, 0)
+    lax.fori_loop(0, ny, send_back_ring, 0)
+    for cy in far_y:
+        send_back(cy, z)
     got3[pl.ds(place, 1)] = msg3[pl.ds(place, 1)]
     by_row = one_hot(line == ((lane // 2) % 2) * heads + (lane // 4) * 2 + lane % 2)
     pltpu.make_async_copy(
@@ -286,20 +333,20 @@
     slots = cache.shape[1]
     vhead = value_up.shape[2]
     padded = -(-(width + 1) // 128) * 128
-    half = rope // 2
-    frequency = np.float32(10000.0) ** (-np.arange(half, dtype=np.float32) / np.float32(half))
-    frequency = np.broadcast_to(frequency.astype(np.float32)[:, None], (half, prompt))
 
     vmem = pl.BlockSpec(memory_space=pltpu.VMEM)
-    smem = pl.BlockSpec(memory_space=pltpu.SMEM)
-    hbm = pl.BlockSpec(memory_space=pl.ANY)
+    hbm = pl.BlockSpec(memory_space=pltpu.HBM)
     dma = pltpu.SemaphoreType.DMA
     return pl.pallas_call(
         functools.partial(kernel, nx, ny, nz, lat, rope),
         out_shape=jax.ShapeDtypeStruct((rows, heads, vhead), bf16),
-        in_specs=[vmem, vmem, vmem, vmem, smem, hbm, hbm, hbm, hbm],
+        in_specs=[hbm] * 8,
         out_specs=vmem,
         scratch_shapes=[
+            pltpu.VMEM((1, lat), f32),
+            pltpu.VMEM((1, prompt), jnp.int32),
+            pltpu.VMEM((1, prompt), jnp.int32),
+            pltpu.SMEM((rows,), jnp.int32),
             pltpu.VMEM((padded, prompt), bf16),
             pltpu.VMEM((rows, width, heads), bf16),
             pltpu.VMEM((rows, width, slots), bf16),
@@ -313,7 +360,7 @@
             pltpu.VMEM((places, 4, lat), bf16),
             pltpu.VMEM((places, 4, vhead), bf16),
             pltpu.VMEM((places, 4, vhead), bf16),
-            dma((4,)),
+            dma((8,)),
             dma, dma, dma, dma,
             dma, dma, dma, dma, dma, dma,
             pltpu.SemaphoreType.REGULAR,
@@ -323,7 +370,6 @@
         ),
         name="serve_window",
     )(
-        jnp.asarray(frequency),
         kv_gain.reshape(1, lat),
         send_list.reshape(1, prompt),
         row_owner.reshape(1, prompt),

time: 62.1 us -> 55.7 us (0.90); the launches traced: 61.9 us -> 54.9 us
  Pallas kernels: 59.1 us -> 53.4 us
  local copies, waits for them, and re-layouts: 2.83 us -> 1.47 us
    pallas_call x1, Pallas kernels: 59.1 us -> 53.4 us  [body(): pl.pallas_call(functools.partial(kernel, nx, ny, nz, lat, rope), out_shap...]
    another operation x1 -> x0, local copies, waits for them, and re-layouts: 1.36 us -> none
where the time goes in v2:
time: 55.7 us; the launch traced here: 54.9 us
  Pallas kernels  53.4 us (96%)
  local copies, waits for them, and re-layouts  1.47 us (3%)
    pallas_call x1, Pallas kernels, body(): pl.pallas_call(functools.partial(kernel, nx, ny, nz, lat, rope), out_shap...  53.4 us
    unnamed x1, local copies, waits for them, and re-layouts  1.47 us

profile of v2, /device:TPU:1, one launch (start us, length us, event | category | flops | bytes accessed | tf_op | source)
XLA Modules:
  0.0 54.9 jit_solution(10656247436985642905)
XLA Ops:
  0.0 53.4 %serve_window.1 = bf16[2,128,128]{2,1,0:T(8,128)(2,1)} custom-call(f32[1,512]{1,0:T(1,128)} %bitcast.9, s32[1,512]{1,0:T(1,128)} %bitcast.10, s32[1,512]{1,0:T(1,128)} %bitcast.11, s32[2]{0:T(128)} %len_hbm.1, bf16[576,512]{1,0:T(8,128)(2,1)} %bitcast.7, bf16[2,576,128]{2,1,0:T(8,128)(2,1)} %bitcast.8, bf16[2,576,1024]{2,1,0:T(8,128)(2,1)} %bitcast.6, ...), custom_call_target="tpu_custom_call" | custom-call | tf_op jit(solution)/shard_map/serve_window/pallas_call | solution.py:340
  53.4 1.5 %copy.10 = bf16[2,128,128]{2,1,0:T(8,128)(2,1)} copy(bf16[2,128,128]{2,1,0:T(8,128)(2,1)} %serve_window.1) | data formatting | bytes 131072

commit v3 on v2

--- a/solution.py
+++ b/solution.py
@@ -23,9 +23,10 @@
     return size // 2 + lax.div(step + 1, 2) * (1 - 2 * lax.rem(step, 2))
 
 
-def moved(position, step, size):
-    place = position + far_first(step, size)
-    return jnp.where(place >= size, place - size, place)
+def moved(position, step, size, way):
+    place = position + way * far_first(step, size)
+    place = jnp.where(place >= size, place - size, place)
+    return jnp.where(place < 0, place + size, place)
 
 
 def dot_nn(a, b):
@@ -58,6 +59,7 @@
     y = lax.div(ep, 2 * nz)
     z = lax.div(lax.rem(ep, 2 * nz), 2)
     core = lax.rem(ep, 2)
+    way = 1 - 2 * core
     chip = (x * ny + y) * nz + z
     place = y * nz + z
     chips = nx * ny * nz
@@ -74,14 +76,14 @@
 
     barrier = pltpu.get_barrier_semaphore()
 
-    far_y = [moved(y, step, ny) for step in range(ny - 1)]
-    far_z = [moved(z, step, nz) for step in range(nz - 1)]
+    far_y = [moved(y, step, ny, way) for step in range(ny - 1)]
+    far_z = [moved(z, step, nz, way) for step in range(nz - 1)]
 
     def greet(cx, cy, cz):
         pl.semaphore_signal(barrier, inc=1, device_id=device(cx, cy, cz), device_id_type=MESH)
 
     def greet_plane(step, carry):
-        cx = moved(x, step, nx)
+        cx = moved(x, step, nx, way)
         for cy in far_y + [y]:
             greet(cx, cy, z)
         return carry
@@ -186,7 +188,7 @@
         ).start()
 
     def send_plane(step, carry):
-        cx = moved(x, step, nx)
+        cx = moved(x, step, nx, way)
         for cy in far_y + [y]:
             send_row(cx, cy, z)
         return carry
@@ -198,10 +200,10 @@
     pl.semaphore_wait(plane_sem, nz - 1)
 
     def send_slab(step, carry):
-        cx = moved(x, step, nx)
+        cx = moved(x, step, nx, way)
 
         def send_ring(inner, carry):
-            cy = moved(y, inner, ny)
+            cy = moved(y, inner, ny, way)
             for cz in far_z:
                 send_row(cx, cy, cz)
             return carry
@@ -258,53 +260,59 @@
     by_chip = one_hot(lane == ((line // 2) % 2) * heads + (line // 4) * 2 + line % 2)
     msg2[...] = dot_nn(by_chip, attended).astype(bf16).reshape(places, 4, lat)
 
-    def send_heads(cy, cz):
-        pltpu.make_async_remote_copy(
-            src_ref=msg2.at[cy * nz + cz], dst_ref=got2.at[place],
-            send_sem=send2, recv_sem=recv2, device_id=device(x, cy, cz), device_id_type=MESH,
-        ).start()
-
-    def send_heads_ring(step, carry):
-        cy = moved(y, step, ny)
-        for cz in far_z:
-            send_heads(cy, cz)
-        return carry
-
-    lax.fori_loop(0, ny, send_heads_ring, 0)
-    for cy in far_y:
-        send_heads(cy, z)
-    got2[pl.ds(place, 1)] = msg2[pl.ds(place, 1)]
+    groups = [(0, 3), (3, ny - 3), (ny - 3, ny)] if ny == 8 else [(0, ny)]
+
+    def exchange(group, source, target, send_sem, recv_sem):
+        def send(cy, cz):
+            pltpu.make_async_remote_copy(
+                src_ref=source.at[cy * nz + cz], dst_ref=target.at[place],
+                send_sem=send_sem, recv_sem=recv_sem.at[group],
+                device_id=device(x, cy, cz), device_id_type=MESH,
+            ).start()
+
+        def send_ring(step, carry):
+            cy = moved(y, step, ny, way)
+            for cz in far_z + [z]:
+                send(cy, cz)
+            return carry
+
+        start, stop = groups[group]
+        last = stop == ny
+        lax.fori_loop(start, stop - 1 if last else stop, send_ring, 0)
+        if last:
+            for cz in far_z:
+                send(y, cz)
+            target[pl.ds(place, 1)] = source[pl.ds(place, 1)]
+
+    def arrival(group, source, target, recv_sem):
+        start, stop = groups[group]
+        count = (stop - start) * nz - (1 if stop == ny else 0)
+        pltpu.make_async_copy(
+            source.at[pl.ds(0, count)], target.at[pl.ds(0, count)], recv_sem.at[group]
+        ).wait()
+
+    for group in range(len(groups)):
+        exchange(group, msg2, got2, send2, recv2)
     swap_value.wait()
     weights = jnp.concatenate([value[0], value[1]], axis=1)
-    pltpu.make_async_copy(
-        msg2.at[pl.ds(0, places - 1)], got2.at[pl.ds(0, places - 1)], recv2
-    ).wait()
     vhead = value.shape[2]
-    projected = dot_nn(got2[...].reshape(4 * places, lat), weights)
-    even = iota((4 * places, vhead), 0) % 2 == 0
-    mine = jnp.where(even, projected[:, :vhead], projected[:, vhead:])
-    msg3[...] = mine.astype(bf16).reshape(places, 4, vhead)
-
-    def send_back(cy, cz):
-        pltpu.make_async_remote_copy(
-            src_ref=msg3.at[cy * nz + cz], dst_ref=got3.at[place],
-            send_sem=send3, recv_sem=recv3, device_id=device(x, cy, cz), device_id_type=MESH,
-        ).start()
-
-    def send_back_ring(step, carry):
-        cy = moved(y, step, ny)
-        for cz in far_z:
-            send_back(cy, cz)
-        return carry
-
-    lax.fori_loop(0, ny, send_back_ring, 0)
-    for cy in far_y:
-        send_back(cy, z)
-    got3[pl.ds(place, 1)] = msg3[pl.ds(place, 1)]
+    for group in range(len(groups)):
+        arrival(group, msg2, got2, recv2)
+        rings = [moved(y, step, ny, way) for step in range(*groups[group])]
+        arrived = jnp.concatenate(
+            [got2[pl.ds(cy * nz, nz)].reshape(4 * nz, lat) for cy in rings], axis=0
+        )
+        projected = dot_nn(arrived, weights)
+        even = lax.rem(iota((arrived.shape[0], vhead), 0), 2) == 0
+        mine = jnp.where(even, projected[:, :vhead], projected[:, vhead:])
+        mine = mine.astype(bf16).reshape(len(rings) * nz, 4, vhead)
+        for index, cy in enumerate(rings):
+            msg3[pl.ds(cy * nz, nz)] = mine[index * nz : (index + 1) * nz]
+        exchange(group, msg3, got3, send3, recv3)
+
     by_row = one_hot(line == ((lane // 2) % 2) * heads + (lane // 4) * 2 + lane % 2)
-    pltpu.make_async_copy(
-        msg3.at[pl.ds(0, places - 1)], got3.at[pl.ds(0, places - 1)], recv3
-    ).wait()
+    for group in range(len(groups)):
+        arrival(group, msg3, got3, recv3)
     out_ref[...] = (
         dot_nn(by_row, got3[...].reshape(4 * places, vhead)).astype(bf16).reshape(2, heads, vhead)
     )
@@ -362,7 +370,7 @@
             pltpu.VMEM((places, 4, vhead), bf16),
             dma((8,)),
             dma, dma, dma, dma,
-            dma, dma, dma, dma, dma, dma,
+            dma, dma, dma, dma((3,)), dma, dma((3,)),
             pltpu.SemaphoreType.REGULAR,
         ],
         compiler_params=pltpu.CompilerParams(

time: 55.7 us -> 55.8 us (level); the launches traced: 54.9 us -> 55.7 us
  Pallas kernels: 53.4 us -> 54.2 us
    pallas_call x1, Pallas kernels: 53.4 us -> 54.2 us  [body(): pl.pallas_call(functools.partial(kernel, nx, ny, nz, lat, rope), out_shap...]
where the time goes in v3:
time: 55.8 us; the launch traced here: 55.7 us
  Pallas kernels  54.2 us (97%)
  local copies, waits for them, and re-layouts  1.47 us (3%)
    pallas_call x1, Pallas kernels, body(): pl.pallas_call(functools.partial(kernel, nx, ny, nz, lat, rope), out_shap...  54.2 us
    unnamed x1, local copies, waits for them, and re-layouts  1.47 us

profile of v3, /device:TPU:1, one launch (start us, length us, event | category | flops | bytes accessed | tf_op | source)
XLA Modules:
  0.0 55.7 jit_solution(17282063385635001789)
XLA Ops:
  0.0 54.2 %serve_window.1 = bf16[2,128,128]{2,1,0:T(8,128)(2,1)} custom-call(f32[1,512]{1,0:T(1,128)} %bitcast.9, s32[1,512]{1,0:T(1,128)} %bitcast.10, s32[1,512]{1,0:T(1,128)} %bitcast.11, s32[2]{0:T(128)} %len_hbm.1, bf16[576,512]{1,0:T(8,128)(2,1)} %bitcast.7, bf16[2,576,128]{2,1,0:T(8,128)(2,1)} %bitcast.8, bf16[2,576,1024]{2,1,0:T(8,128)(2,1)} %bitcast.6, ...), custom_call_target="tpu_custom_call" | custom-call | tf_op jit(solution)/shard_map/serve_window/pallas_call | solution.py:348
  54.2 1.5 %copy.10 = bf16[2,128,128]{2,1,0:T(8,128)(2,1)} copy(bf16[2,128,128]{2,1,0:T(8,128)(2,1)} %serve_window.1) | data formatting | bytes 131072

commit v4 on v3

--- a/solution.py
+++ b/solution.py
@@ -181,44 +181,53 @@
     both = own_rows.astype(f32) + dot_nn(spread, core_in[...])
     msg1[...] = both.astype(bf16).reshape(chips, 2, padded)
 
-    def send_row(cx, cy, cz):
+    def send_row(cx, cy, cz, near):
         pltpu.make_async_remote_copy(
             src_ref=msg1.at[(cx * ny + cy) * nz + cz], dst_ref=got1.at[chip],
-            send_sem=send1, recv_sem=recv1, device_id=device(cx, cy, cz), device_id_type=MESH,
+            send_sem=send1, recv_sem=recv1.at[near], device_id=device(cx, cy, cz), device_id_type=MESH,
         ).start()
 
     def send_plane(step, carry):
         cx = moved(x, step, nx, way)
         for cy in far_y + [y]:
-            send_row(cx, cy, z)
+            send_row(cx, cy, z, 0)
         return carry
 
     lax.fori_loop(0, nx - 1, send_plane, 0)
     for cy in far_y:
-        send_row(x, cy, z)
+        send_row(x, cy, z, 1)
 
     pl.semaphore_wait(plane_sem, nz - 1)
 
-    def send_slab(step, carry):
-        cx = moved(x, step, nx, way)
-
+    def send_slab(cx, near):
         def send_ring(inner, carry):
             cy = moved(y, inner, ny, way)
             for cz in far_z:
-                send_row(cx, cy, cz)
+                send_row(cx, cy, cz, near)
             return carry
 
-        return lax.fori_loop(0, ny, send_ring, carry)
-
-    lax.fori_loop(0, nx, send_slab, 0)
+        lax.fori_loop(0, ny, send_ring, 0)
+
+    def send_far_slab(step, carry):
+        send_slab(moved(x, step, nx, way), 0)
+        return carry
+
+    lax.fori_loop(0, nx - 1, send_far_slab, 0)
+    send_slab(x, 1)
     got1[pl.ds(chip, 1)] = msg1[pl.ds(chip, 1)]
 
     load_query.wait()
     unit = one_hot(iota((heads, heads), 0) == iota((heads, heads), 1))
-    for r in range(2):
-        qpad[r * heads : (r + 1) * heads, :] = jnp.concatenate(
-            [dot_nt(unit, query_t[r]), jnp.zeros((heads, tail), f32)], axis=1
-        ).astype(bf16)
+    line = iota((2 * heads, 2 * heads), 0)
+    lane = iota((2 * heads, 2 * heads), 1)
+    by_chip = one_hot(
+        lane == lax.rem(lax.div(line, 2), 2) * heads + lax.div(line, 4) * 2 + lax.rem(line, 2)
+    )
+    query = [dot_nt(unit, query_t[r]).astype(bf16) for r in range(2)]
+    ordered = dot_nn(by_chip, jnp.concatenate(query, axis=0))
+    qpad[: 2 * heads, :] = jnp.concatenate(
+        [ordered, jnp.zeros((2 * heads, tail), f32)], axis=1
+    ).astype(bf16)
     qpad[2 * heads : 2 * heads + 16, :] = one_hot(
         jnp.logical_and(iota((16, padded), 0) == 0, iota((16, padded), 1) == width)
     )
@@ -227,38 +236,59 @@
     load_len.wait()
     peaks, sums, totals = [], [], []
     for r in range(2):
-        scores = dot_nn(qpad[r * heads : (r + 1) * heads, :width], cache[r]) * score_scale
+        scores = dot_nn(query[r], cache[r]) * score_scale
         scores = jnp.where(iota(scores.shape, 1) < len_ref[r], scores, masked)
         peak = jnp.max(scores, axis=1, keepdims=True)
         weight = jnp.exp(scores - peak)
         peaks.append(peak)
         sums.append(jnp.sum(weight, axis=1, keepdims=True))
         totals.append(dot_nt(weight.astype(bf16), cache[r, :lat, :]))
-    peak_cache = jnp.concatenate(peaks, axis=0)
-    sum_cache = jnp.concatenate(sums, axis=0)
-    total_cache = jnp.concatenate(totals, axis=0)
-
-    all_rows = pltpu.make_async_copy(
-        msg1.at[pl.ds(0, chips - 1)], got1.at[pl.ds(0, chips - 1)], recv1
-    )
-    all_rows.wait()
-    fresh = got1[...].reshape(2 * chips, padded)
-    raw = dot_nt(qpad[...], fresh)
+    side = jnp.where(
+        iota((2 * heads, 128), 1) == 0,
+        jnp.concatenate(peaks, axis=0),
+        jnp.concatenate(sums, axis=0),
+    )
+    held = jnp.dot(
+        by_chip.astype(f32),
+        jnp.concatenate([jnp.concatenate(totals, axis=0), side], axis=1),
+        precision=lax.Precision.HIGHEST,
+        preferred_element_type=f32,
+    )
+    total_cache = held[:, :lat]
+    peak_cache = held[:, lat : lat + 1]
+    sum_cache = held[:, lat + 1 : lat + 2]
+
+    far_count = (nx - 1) * places
+    pltpu.make_async_copy(
+        msg1.at[pl.ds(0, far_count)], got1.at[pl.ds(0, far_count)], recv1.at[0]
+    ).wait()
+    slabs = [lax.rem(x + step, nx) for step in range(1, nx)]
+    far_keys = jnp.concatenate(
+        [got1[pl.ds(cx * places, places)].reshape(2 * places, padded) for cx in slabs], axis=0
+    )
+    far_raw = dot_nt(qpad[...], far_keys)
+    pltpu.make_async_copy(
+        msg1.at[pl.ds(0, places - 1)], got1.at[pl.ds(0, places - 1)], recv1.at[1]
+    ).wait()
+    near_keys = got1[pl.ds(x * places, places)].reshape(2 * places, padded)
+    raw = jnp.concatenate([far_raw, dot_nt(qpad[...], near_keys)], axis=1)
     owner = raw[2 * heads : 2 * heads + 1, :]
     scores = raw[: 2 * heads, :] * score_scale
-    row = (iota(scores.shape, 0) // heads).astype(f32)
+    row = lax.rem(lax.div(iota(scores.shape, 0), 2), 2).astype(f32)
     scores = jnp.where(row == owner, scores, masked)
     peak = jnp.maximum(peak_cache, jnp.max(scores, axis=1, keepdims=True))
     weight = jnp.exp(scores - peak)
     scale_cache = jnp.exp(peak_cache - peak)
     denominator = sum_cache * scale_cache + jnp.sum(weight, axis=1, keepdims=True)
-    total = total_cache * scale_cache + dot_nn(weight.astype(bf16), fresh[:, :lat])
-    attended = (total / denominator).astype(bf16)
-
-    line = iota((2 * heads, 2 * heads), 0)
-    lane = iota((2 * heads, 2 * heads), 1)
-    by_chip = one_hot(lane == ((line // 2) % 2) * heads + (line // 4) * 2 + line % 2)
-    msg2[...] = dot_nn(by_chip, attended).astype(bf16).reshape(places, 4, lat)
+    weight = weight.astype(bf16)
+    split = 2 * far_count
+    total = (
+        total_cache * scale_cache
+        + dot_nn(weight[:, :split], far_keys[:, :lat])
+        + dot_nn(weight[:, split:], near_keys[:, :lat])
+    )
+
+    msg2[...] = (total / denominator).astype(bf16).reshape(places, 4, lat)
 
     groups = [(0, 3), (3, ny - 3), (ny - 3, ny)] if ny == 8 else [(0, ny)]
 
@@ -370,7 +400,7 @@
             pltpu.VMEM((places, 4, vhead), bf16),
             dma((8,)),
             dma, dma, dma, dma,
-            dma, dma, dma, dma((3,)), dma, dma((3,)),
+            dma, dma((2,)), dma, dma((3,)), dma, dma((3,)),
             pltpu.SemaphoreType.REGULAR,
         ],
         compiler_params=pltpu.CompilerParams(

time: 55.8 us -> 55.4 us (level)
  no operation moved by 1% of the time
where the time goes in v4:
time: 55.4 us; the launch traced here: 55.3 us
  Pallas kernels  53.8 us (97%)
  local copies, waits for them, and re-layouts  1.47 us (3%)
    pallas_call x1, Pallas kernels, body(): pl.pallas_call(functools.partial(kernel, nx, ny, nz, lat, rope), out_shap...  53.8 us
    unnamed x1, local copies, waits for them, and re-layouts  1.47 us

profile of v4, /device:TPU:1, one launch (start us, length us, event | category | flops | bytes accessed | tf_op | source)
XLA Modules:
  0.0 55.3 jit_solution(16779972015953296020)
XLA Ops:
  0.0 53.8 %serve_window.1 = bf16[2,128,128]{2,1,0:T(8,128)(2,1)} custom-call(f32[1,512]{1,0:T(1,128)} %bitcast.9, s32[1,512]{1,0:T(1,128)} %bitcast.10, s32[1,512]{1,0:T(1,128)} %bitcast.11, s32[2]{0:T(128)} %len_hbm.1, bf16[576,512]{1,0:T(8,128)(2,1)} %bitcast.7, bf16[2,576,128]{2,1,0:T(8,128)(2,1)} %bitcast.8, bf16[2,576,1024]{2,1,0:T(8,128)(2,1)} %bitcast.6, ...), custom_call_target="tpu_custom_call" | custom-call | tf_op jit(solution)/shard_map/serve_window/pallas_call | solution.py:378
  53.8 1.5 %copy.10 = bf16[2,128,128]{2,1,0:T(8,128)(2,1)} copy(bf16[2,128,128]{2,1,0:T(8,128)(2,1)} %serve_window.1) | data formatting | bytes 131072
